TPU v7x, 32 devices: a whole 2x2x4 slice. The times are simulated.
32 devices in a mesh: bx: 8 (over z, y), by: 4 (over x, core).
Axes of the slice: x: 2, y: 2, z: 4, core: 2. Of those that a mesh axis runs over, the one named last changes fastest.
Arguments:
- source: bfloat16 [8, 4, 2, 128, 1024], P('bx', 'by'), may hold values from -6 to 6
- start_tick: int32 [8, 4], P('bx', 'by'), may hold values from 0 to 3, as said below
- op_x: bfloat16 [8, 4, 2, 1024, 1024], P('bx', 'by'), may hold values from -0.09375 to 0.09375
- op_y: bfloat16 [8, 4, 2, 1024, 1024], P('bx', 'by'), may hold values from -0.09375 to 0.09375
Outputs:
- upgoing: float32 [4, 128, 2, 8, 1024], P('by', 'bx')
Inputs may be any that keep to these rules, and one draw needn't show every extreme that they name: `start_tick`: both 0 and 3 occur in every draw.
All inputs are finite; a program needn't handle non-finite values.
Results may differ from a plain program's by a relative error of at most 0.012.
Values may be sent and summed in bfloat16 or wider, within the bound.
A program may use at most 64 MiB of HBM per device.

v0:
```python
import math

import jax
import jax.numpy as jnp
from jax import lax
from jax.sharding import PartitionSpec as P

F = 1024
TICKS = 4


def passed_along(value, axis, by):
    peers = lax.axis_size(axis)
    pairs = [(i, i + by) for i in range(peers) if 0 <= i + by < peers]
    return lax.ppermute(value, axis, pairs)


def dft_tables(length):
    indices = jnp.arange(length, dtype=jnp.int32)
    products = indices[:, None] * indices[None, :] % length
    angles = products.astype(jnp.float32) * (2.0 * math.pi / length)
    return (jnp.cos(angles).astype(jnp.bfloat16), jnp.sin(angles).astype(jnp.bfloat16))


def complex_apply(traces, operator):
    shot_count = traces.shape[1]
    stacked = traces.reshape(2 * shot_count, traces.shape[2])
    with_real = jnp.dot(stacked, operator[0], preferred_element_type=jnp.float32)
    with_imag = jnp.dot(stacked, operator[1], preferred_element_type=jnp.float32)
    real_out = with_real[:shot_count] - with_imag[shot_count:]
    imag_out = with_imag[:shot_count] + with_real[shot_count:]
    return jnp.stack([real_out, imag_out])


def line_spectrum(values, cos_line, sin_line):
    old_shape = values.shape
    flattened = values.reshape(2, -1, old_shape[-1])
    row_count = flattened.shape[1]
    stacked = flattened.reshape(2 * row_count, old_shape[-1])
    cosine_part = jnp.dot(stacked, cos_line, preferred_element_type=jnp.float32)
    sine_part = jnp.dot(stacked, sin_line, preferred_element_type=jnp.float32)
    real_out = cosine_part[:row_count] + sine_part[row_count:]
    imag_out = cosine_part[row_count:] - sine_part[:row_count]
    return jnp.stack([real_out, imag_out]).reshape(old_shape).astype(jnp.bfloat16)


def shards(source, start_tick, op_x, op_y):
    local_source = source[0, 0].astype(jnp.float32)
    operator_x = op_x[0, 0]
    operator_y = op_y[0, 0]
    first_tick = start_tick[0, 0]
    shot_count = local_source.shape[1]
    east_out = None
    north_out = None
    for tick in range(TICKS):
        active = (first_tick <= tick).astype(jnp.float32)
        if tick == 0:
            incident = (active * local_source).astype(jnp.bfloat16)
        else:
            from_west = passed_along(east_out, "bx", 1)
            from_south = passed_along(north_out, "by", 1)
            incident = (
                from_west.astype(jnp.float32)
                + from_south.astype(jnp.float32)
                + active * local_source
            ).astype(jnp.bfloat16)
        east_out = complex_apply(incident, operator_x).astype(jnp.bfloat16)
        north_out = complex_apply(incident, operator_y).astype(jnp.bfloat16)
    from_west = passed_along(east_out, "bx", 1)
    from_east = passed_along(east_out, "bx", -1)
    from_south = passed_along(north_out, "by", 1)
    from_north = passed_along(north_out, "by", -1)
    mismatch = (
        from_west.astype(jnp.float32)
        + from_south.astype(jnp.float32)
        - from_east.astype(jnp.float32)
        - from_north.astype(jnp.float32)
    ).astype(jnp.bfloat16)
    reflected = complex_apply(mismatch, operator_x).astype(jnp.bfloat16)
    cos_line, sin_line = dft_tables(F)
    pieces = lax.axis_size("bx")
    owned = shot_count // pieces
    arranged = reflected.reshape(2, pieces, owned, 1, F)
    regrouped = line_spectrum(
        lax.all_to_all(arranged, "bx", split_axis=1, concat_axis=3, tiled=True), cos_line, sin_line
    )
    spectrum = regrouped.reshape(2, owned, pieces, F)
    cos_grid, sin_grid = dft_tables(pieces)
    out_real = jnp.einsum(
        "sik,iq->sqk", spectrum[0], cos_grid, preferred_element_type=jnp.float32
    ) + jnp.einsum("sik,iq->sqk", spectrum[1], sin_grid, preferred_element_type=jnp.float32)
    out_imag = jnp.einsum(
        "sik,iq->sqk", spectrum[1], cos_grid, preferred_element_type=jnp.float32
    ) - jnp.einsum("sik,iq->sqk", spectrum[0], sin_grid, preferred_element_type=jnp.float32)
    wave_index = jnp.arange(pieces, dtype=jnp.int32)
    signed = jnp.where(wave_index < pieces // 2, wave_index, wave_index - pieces).astype(
        jnp.float32
    )
    weights = 0.5 * (1.0 + signed / jnp.sqrt(signed * signed + 1.0))
    upgoing = jnp.stack([out_real, out_imag], axis=1) * weights[None, None, :, None]
    return upgoing.reshape((1,) + upgoing.shape)


def solution(mesh):
    placed = (
        P("bx", "by", None, None, None),
        P("bx", "by"),
        P("bx", "by", None, None, None),
        P("bx", "by", None, None, None),
    )
    return jax.shard_map(
        shards,
        mesh=mesh,
        in_specs=placed,
        out_specs=P("by", "bx", None, None, None),
        check_vma=False,
    )
```

profile of v0, /device:TPU:4, one launch (start us, length us, event | category | flops | bytes accessed | tf_op | source)
XLA Modules:
  0.0 144.0 jit_solution(1058366480971827161)
XLA Ops:
  0.8 1.3 fusion.66
  2.1 2.3 %fusion.32 = f32[256,1024]{1,0:T(8,128)S(1)} fusion(bf16[256,1024]{1,0:T(8,128)(2,1)S(1)} %bitcast.172, bf16[1,1,2,1024,1024]{4,3,2,1,0:T(8,128)(2,1)} %param.6), kind=kOutput, calls=%fused_computation.37 | convolution fusion | flops 536870912 | bytes 3670016 | tf_op jit(solution)/shard_map/dot_general | solution.py:29
  4.4 0.7 fusion.42
  5.4 3.6 %collective-permute-start = (bf16[2,128,1024]{2,1,0:T(8,128)(2,1)S(1)}, bf16[2,128,1024]{2,1,0:T(8,128)(2,1)S(1)}, u32[]{:S(2)}, u32[]{:S(2)}) collective-permute-start(bf16[2,128,1024]{2,1,0:T(8,128)(2,1)S(1)} %pad_maximum_fusion), channel_id=1, source_target_pairs={{0,4},{4,8},{8,12},{12,16},{16,20},{20,24},{24,28},{1,5},{5,9},{9,... | collective-permute-start | bytes 1572872 | tf_op jit(solution)/shard_map/ppermute | solution.py:15
  9.0 0.7 fusion.14
  9.7 0.7 fusion.22
  10.7 1.5 %collective-permute-start.1 = (bf16[2,128,1024]{2,1,0:T(8,128)(2,1)S(1)}, bf16[2,128,1024]{2,1,0:T(8,128)(2,1)S(1)}, u32[]{:S(2)}, u32[]{:S(2)}) collective-permute-start(bf16[2,128,1024]{2,1,0:T(8,128)(2,1)S(1)} %pad_maximum_fusion.1), channel_id=1, source_target_pairs={{0,1},{1,2},{2,3},{4,5},{5,6},{6,7},{8,9},{9,10},{10,11},{12,13},{... | collective-permute-start | bytes 1572872 | tf_op jit(solution)/shard_map/ppermute | solution.py:15
  12.2 8.9 %collective-permute-done = bf16[2,128,1024]{2,1,0:T(8,128)(2,1)S(1)} collective-permute-done((bf16[2,128,1024]{2,1,0:T(8,128)(2,1)S(1)}, bf16[2,128,1024]{2,1,0:T(8,128)(2,1)S(1)}, u32[]{:S(2)}, u32[]{:S(2)}) %collective-permute-start) | collective-permute-done | bytes 524320 | tf_op jit(solution)/shard_map/ppermute | solution.py:15
  21.1 0.3 fusion.69
  21.4 0.7 fusion.30
  22.1 0.7 fusion.40
  22.8 0.7 fusion.12
  23.6 0.7 fusion.20
  24.5 4.3 %collective-permute-start.2 = (bf16[2,128,1024]{2,1,0:T(8,128)(2,1)S(1)}, bf16[2,128,1024]{2,1,0:T(8,128)(2,1)S(1)}, u32[]{:S(2)}, u32[]{:S(2)}) collective-permute-start(bf16[2,128,1024]{2,1,0:T(8,128)(2,1)S(1)} %pad_maximum_fusion.2), channel_id=1, source_target_pairs={{0,4},{4,8},{8,12},{12,16},{16,20},{20,24},{24,28},{1,5},{5,9},{9,... | collective-permute-start | bytes 1572872 | tf_op jit(solution)/shard_map/ppermute | solution.py:15
  29.2 1.3 collective-permute-start.3
  30.5 9.0 %collective-permute-done.2 = bf16[2,128,1024]{2,1,0:T(8,128)(2,1)S(1)} collective-permute-done((bf16[2,128,1024]{2,1,0:T(8,128)(2,1)S(1)}, bf16[2,128,1024]{2,1,0:T(8,128)(2,1)S(1)}, u32[]{:S(2)}, u32[]{:S(2)}) %collective-permute-start.2) | collective-permute-done | bytes 524320 | tf_op jit(solution)/shard_map/ppermute | solution.py:15
  39.5 0.3 fusion.72
  39.8 0.7 fusion.28
  40.5 0.7 fusion.38
  41.2 0.7 fusion.10
  41.9 0.7 fusion.18
  42.9 5.0 %collective-permute-start.4 = (bf16[2,128,1024]{2,1,0:T(8,128)(2,1)S(1)}, bf16[2,128,1024]{2,1,0:T(8,128)(2,1)S(1)}, u32[]{:S(2)}, u32[]{:S(2)}) collective-permute-start(bf16[2,128,1024]{2,1,0:T(8,128)(2,1)S(1)} %pad_maximum_fusion.4), channel_id=1, source_target_pairs={{0,4},{4,8},{8,12},{12,16},{16,20},{20,24},{24,28},{1,5},{5,9},{9,... | collective-permute-start | bytes 1572872 | tf_op jit(solution)/shard_map/ppermute | solution.py:15
  48.1 1.3 collective-permute-start.5
  49.5 8.4 %collective-permute-done.4 = bf16[2,128,1024]{2,1,0:T(8,128)(2,1)S(1)} collective-permute-done((bf16[2,128,1024]{2,1,0:T(8,128)(2,1)S(1)}, bf16[2,128,1024]{2,1,0:T(8,128)(2,1)S(1)}, u32[]{:S(2)}, u32[]{:S(2)}) %collective-permute-start.4) | collective-permute-done | bytes 524320 | tf_op jit(solution)/shard_map/ppermute | solution.py:15
  57.9 0.3 fusion.75
  58.2 0.7 fusion.26
  58.9 0.7 fusion.36
  59.9 4.6 %collective-permute-start.6 = (bf16[2,128,1024]{2,1,0:T(8,128)(2,1)S(1)}, bf16[2,128,1024]{2,1,0:T(8,128)(2,1)S(1)}, u32[]{:S(2)}, u32[]{:S(2)}) collective-permute-start(bf16[2,128,1024]{2,1,0:T(8,128)(2,1)S(1)} %pad_maximum_fusion.6), channel_id=1, source_target_pairs={{0,4},{4,8},{8,12},{12,16},{16,20},{20,24},{24,28},{1,5},{5,9},{9,... | collective-permute-start | bytes 1572872 | tf_op jit(solution)/shard_map/ppermute | solution.py:15
  64.5 2.1 %collective-permute-start.8 = (bf16[2,128,1024]{2,1,0:T(8,128)(2,1)S(1)}, bf16[2,128,1024]{2,1,0:T(8,128)(2,1)S(1)}, u32[]{:S(2)}, u32[]{:S(2)}) collective-permute-start(bf16[2,128,1024]{2,1,0:T(8,128)(2,1)S(1)} %pad_maximum_fusion.6), channel_id=1, source_target_pairs={{4,0},{8,4},{12,8},{16,12},{20,16},{24,20},{28,24},{5,1},{9,5},{13... | collective-permute-start | bytes 1572872 | tf_op jit(solution)/shard_map/ppermute | solution.py:15
  66.6 0.7 fusion.16
  67.4 0.7 fusion.8
  68.3 1.3 collective-permute-start.7
  69.7 1.3 collective-permute-start.9
  71.0 15.8 %collective-permute-done.6 = bf16[2,128,1024]{2,1,0:T(8,128)(2,1)S(1)} collective-permute-done((bf16[2,128,1024]{2,1,0:T(8,128)(2,1)S(1)}, bf16[2,128,1024]{2,1,0:T(8,128)(2,1)S(1)}, u32[]{:S(2)}, u32[]{:S(2)}) %collective-permute-start.6) | collective-permute-done | bytes 524320 | tf_op jit(solution)/shard_map/ppermute | solution.py:15
  86.7 0.4 subtract_convert_fusion
  87.1 0.7 fusion.24
  87.8 0.7 fusion.34
  88.7 0.8 pad_maximum_fusion.8
  89.6 5.3 %all-to-all-start = ((bf16[2,8,16,1,1024]{4,2,0,3,1:T(8,128)(2,1)}), bf16[2,8,16,1,1024]{4,2,0,3,1:T(8,128)(2,1)S(1)}, u32[]{:S(2)}, u32[]{:S(2)}) async-start(bf16[2,8,16,1,1024]{4,2,0,3,1:T(8,128)(2,1)} %pad_maximum_fusion.8), calls=%async_computation | async-start | bytes 1048576 | tf_op jit(solution)/shard_map/all_to_all | solution.py:85
  94.9 13.8 %all-to-all-done = bf16[2,8,16,1,1024]{4,2,0,3,1:T(8,128)(2,1)S(1)} async-done(((bf16[2,8,16,1,1024]{4,2,0,3,1:T(8,128)(2,1)}), bf16[2,8,16,1,1024]{4,2,0,3,1:T(8,128)(2,1)S(1)}, u32[]{:S(2)}, u32[]{:S(2)}) %all-to-all-start) | async-done | bytes 524320 | tf_op jit(solution)/shard_map/all_to_all | solution.py:85
  108.7 0.3 copy.11
  109.0 16.1 %fusion.6 = f32[256,1024]{1,0:T(8,128)S(1)} fusion(bf16[256,1024]{1,0:T(8,128)(2,1)S(1)} %bitcast.170), kind=kOutput, calls=%fused_computation.11 | convolution fusion | flops 552599552 | bytes 1572864 | tf_op jit(solution)/shard_map/dot_general | solution.py:40
  125.2 16.3 %fusion.7 = f32[256,1024]{1,0:T(8,128)S(1)} fusion(bf16[256,1024]{1,0:T(8,128)(2,1)S(1)} %bitcast.171), kind=kOutput, calls=%fused_computation.12 | convolution fusion | flops 552599552 | bytes 1572864 | tf_op jit(solution)/shard_map/dot_general | solution.py:41
  141.6 0.3 fusion.126
  141.9 0.3 fusion.124
  142.2 0.3 fusion.54
  142.4 0.3 fusion.55
  142.9 1.1 copy.12
  (32 shorter events, 2.7 us)
Async XLA Ops:
  0.0 4.4 %copy-start.2 = (bf16[1,1,2,1024,1024]{4,3,2,1,0:T(8,128)(2,1)S(1)}, bf16[1,1,2,1024,1024]{4,3,2,1,0:T(8,128)(2,1)}, u32[]{:S(2)}) copy-start(bf16[1,1,2,1024,1024]{4,3,2,1,0:T(8,128)(2,1)} %param.6) | copy-start | bytes 12582916
  4.4 4.6 %copy-start.1 = (bf16[1,1,2,1024,1024]{4,3,2,1,0:T(8,128)(2,1)S(1)}, bf16[1,1,2,1024,1024]{4,3,2,1,0:T(8,128)(2,1)}, u32[]{:S(2)}) copy-start(bf16[1,1,2,1024,1024]{4,3,2,1,0:T(8,128)(2,1)} %param.7) | copy-start | bytes 12582916
  5.4 15.7 %collective-permute-start = (bf16[2,128,1024]{2,1,0:T(8,128)(2,1)S(1)}, bf16[2,128,1024]{2,1,0:T(8,128)(2,1)S(1)}, u32[]{:S(2)}, u32[]{:S(2)}) collective-permute-start(bf16[2,128,1024]{2,1,0:T(8,128)(2,1)S(1)} %pad_maximum_fusion), channel_id=1, source_target_pairs={{0,4},{4,8},{8,12},{12,16},{16,20},{20,24},{24,28},{1,5},{5,9},{9,... | collective-permute-start | bytes 1572872 | tf_op jit(solution)/shard_map/ppermute | solution.py:15
  9.7 11.4 %copy-start = (bf16[1,1,2,128,1024]{4,3,2,1,0:T(8,128)(2,1)S(1)}, bf16[1,1,2,128,1024]{4,3,2,1,0:T(8,128)(2,1)}, u32[]{:S(2)}) copy-start(bf16[1,1,2,128,1024]{4,3,2,1,0:T(8,128)(2,1)} %param.4) | copy-start | bytes 1572868
  10.7 10.4 %collective-permute-start.1 = (bf16[2,128,1024]{2,1,0:T(8,128)(2,1)S(1)}, bf16[2,128,1024]{2,1,0:T(8,128)(2,1)S(1)}, u32[]{:S(2)}, u32[]{:S(2)}) collective-permute-start(bf16[2,128,1024]{2,1,0:T(8,128)(2,1)S(1)} %pad_maximum_fusion.1), channel_id=1, source_target_pairs={{0,1},{1,2},{2,3},{4,5},{5,6},{6,7},{8,9},{9,10},{10,11},{12,13},{... | collective-permute-start | bytes 1572872 | tf_op jit(solution)/shard_map/ppermute | solution.py:15
  24.5 14.9 %collective-permute-start.2 = (bf16[2,128,1024]{2,1,0:T(8,128)(2,1)S(1)}, bf16[2,128,1024]{2,1,0:T(8,128)(2,1)S(1)}, u32[]{:S(2)}, u32[]{:S(2)}) collective-permute-start(bf16[2,128,1024]{2,1,0:T(8,128)(2,1)S(1)} %pad_maximum_fusion.2), channel_id=1, source_target_pairs={{0,4},{4,8},{8,12},{12,16},{16,20},{20,24},{24,28},{1,5},{5,9},{9,... | collective-permute-start | bytes 1572872 | tf_op jit(solution)/shard_map/ppermute | solution.py:15
  29.2 10.3 %collective-permute-start.3 = (bf16[2,128,1024]{2,1,0:T(8,128)(2,1)S(1)}, bf16[2,128,1024]{2,1,0:T(8,128)(2,1)S(1)}, u32[]{:S(2)}, u32[]{:S(2)}) collective-permute-start(bf16[2,128,1024]{2,1,0:T(8,128)(2,1)S(1)} %pad_maximum_fusion.3), channel_id=1, source_target_pairs={{0,1},{1,2},{2,3},{4,5},{5,6},{6,7},{8,9},{9,10},{10,11},{12,13},{... | collective-permute-start | bytes 1572872 | tf_op jit(solution)/shard_map/ppermute | solution.py:15
  42.9 15.0 %collective-permute-start.4 = (bf16[2,128,1024]{2,1,0:T(8,128)(2,1)S(1)}, bf16[2,128,1024]{2,1,0:T(8,128)(2,1)S(1)}, u32[]{:S(2)}, u32[]{:S(2)}) collective-permute-start(bf16[2,128,1024]{2,1,0:T(8,128)(2,1)S(1)} %pad_maximum_fusion.4), channel_id=1, source_target_pairs={{0,4},{4,8},{8,12},{12,16},{16,20},{20,24},{24,28},{1,5},{5,9},{9,... | collective-permute-start | bytes 1572872 | tf_op jit(solution)/shard_map/ppermute | solution.py:15
  48.1 9.8 %collective-permute-start.5 = (bf16[2,128,1024]{2,1,0:T(8,128)(2,1)S(1)}, bf16[2,128,1024]{2,1,0:T(8,128)(2,1)S(1)}, u32[]{:S(2)}, u32[]{:S(2)}) collective-permute-start(bf16[2,128,1024]{2,1,0:T(8,128)(2,1)S(1)} %pad_maximum_fusion.5), channel_id=1, source_target_pairs={{0,1},{1,2},{2,3},{4,5},{5,6},{6,7},{8,9},{9,10},{10,11},{12,13},{... | collective-permute-start | bytes 1572872 | tf_op jit(solution)/shard_map/ppermute | solution.py:15
  59.9 26.8 %collective-permute-start.6 = (bf16[2,128,1024]{2,1,0:T(8,128)(2,1)S(1)}, bf16[2,128,1024]{2,1,0:T(8,128)(2,1)S(1)}, u32[]{:S(2)}, u32[]{:S(2)}) collective-permute-start(bf16[2,128,1024]{2,1,0:T(8,128)(2,1)S(1)} %pad_maximum_fusion.6), channel_id=1, source_target_pairs={{0,4},{4,8},{8,12},{12,16},{16,20},{20,24},{24,28},{1,5},{5,9},{9,... | collective-permute-start | bytes 1572872 | tf_op jit(solution)/shard_map/ppermute | solution.py:15
  64.5 22.2 %collective-permute-start.8 = (bf16[2,128,1024]{2,1,0:T(8,128)(2,1)S(1)}, bf16[2,128,1024]{2,1,0:T(8,128)(2,1)S(1)}, u32[]{:S(2)}, u32[]{:S(2)}) collective-permute-start(bf16[2,128,1024]{2,1,0:T(8,128)(2,1)S(1)} %pad_maximum_fusion.6), channel_id=1, source_target_pairs={{4,0},{8,4},{12,8},{16,12},{20,16},{24,20},{28,24},{5,1},{9,5},{13... | collective-permute-start | bytes 1572872 | tf_op jit(solution)/shard_map/ppermute | solution.py:15
  68.3 18.4 %collective-permute-start.7 = (bf16[2,128,1024]{2,1,0:T(8,128)(2,1)S(1)}, bf16[2,128,1024]{2,1,0:T(8,128)(2,1)S(1)}, u32[]{:S(2)}, u32[]{:S(2)}) collective-permute-start(bf16[2,128,1024]{2,1,0:T(8,128)(2,1)S(1)} %pad_maximum_fusion.7), channel_id=1, source_target_pairs={{0,1},{1,2},{2,3},{4,5},{5,6},{6,7},{8,9},{9,10},{10,11},{12,13},{... | collective-permute-start | bytes 1572872 | tf_op jit(solution)/shard_map/ppermute | solution.py:15
  69.7 17.1 %collective-permute-start.9 = (bf16[2,128,1024]{2,1,0:T(8,128)(2,1)S(1)}, bf16[2,128,1024]{2,1,0:T(8,128)(2,1)S(1)}, u32[]{:S(2)}, u32[]{:S(2)}) collective-permute-start(bf16[2,128,1024]{2,1,0:T(8,128)(2,1)S(1)} %pad_maximum_fusion.7), channel_id=1, source_target_pairs={{1,0},{2,1},{3,2},{5,4},{6,5},{7,6},{9,8},{10,9},{11,10},{13,12},{... | collective-permute-start | bytes 1572872 | tf_op jit(solution)/shard_map/ppermute | solution.py:15
  89.6 19.2 %all-to-all-start = ((bf16[2,8,16,1,1024]{4,2,0,3,1:T(8,128)(2,1)}), bf16[2,8,16,1,1024]{4,2,0,3,1:T(8,128)(2,1)S(1)}, u32[]{:S(2)}, u32[]{:S(2)}) async-start(bf16[2,8,16,1,1024]{4,2,0,3,1:T(8,128)(2,1)} %pad_maximum_fusion.8), calls=%async_computation | async-start | bytes 1048576 | tf_op jit(solution)/shard_map/all_to_all | solution.py:85
where the time goes:
time: 146 us; the launch traced here: 144 us
  waiting for transfers between devices  55.9 us (38%)
  matrix products  47.7 us (33%)
  starting transfers between devices  31.6 us (22%)
  other arithmetic  6 us (4%)
    ppermute x10, waiting for transfers between devices, passed_along(): return lax.ppermute(value, axis, pairs)  42.1 us
    ppermute x10, starting transfers between devices, passed_along(): return lax.ppermute(value, axis, pairs)  26.3 us
    dot_general x1, matrix products, line_spectrum(): sine_part = jnp.dot(stacked, sin_line, preferred_element_type=jnp.float32)  16.3 us
    dot_general x1, matrix products, line_spectrum(): cosine_part = jnp.dot(stacked, cos_line, preferred_element_type=jnp.float32)  16.1 us
    all_to_all x1, waiting for transfers between devices, shards(): lax.all_to_all(arranged, 'bx', split_axis=1, concat_axis=3, tiled=True)  13.8 us
    dot_general x9, matrix products, complex_apply(): jnp.dot(stacked, operator[1], preferred_element_type=jnp.float32)  7.94 us
    dot_general x9, matrix products, complex_apply(): jnp.dot(stacked, operator[0], preferred_element_type=jnp.float32)  6.35 us
    all_to_all x1, starting transfers between devices, shards(): lax.all_to_all(arranged, 'bx', split_axis=1, concat_axis=3, tiled=True)  5.32 us
  transfers between devices with their start and end apart: 11, of which 5 were waited for; matrix products, arithmetic and copies ran while one was open for 3% of the time, Pallas kernels for 0%

commit v1 on v0

v1 whole, which is shorter than its diff:
```python
import functools
import math

import jax
import jax.numpy as jnp
import ml_dtypes
import numpy as np
from jax import lax
from jax.experimental import pallas as pl
from jax.experimental.pallas import tpu as pltpu
from jax.sharding import PartitionSpec as P

TICKS = 4
CHUNKS = 4
MESH = pl.DeviceIdType.MESH
BF16 = jnp.bfloat16
F32 = jnp.float32


def dft_tables(length):
    indices = np.arange(length, dtype=np.int64)
    angles = (indices[:, None] * indices[None, :] % length) * (2.0 * math.pi / length)
    return np.cos(angles).astype(ml_dtypes.bfloat16), np.sin(angles).astype(ml_dtypes.bfloat16)


def grid_gain(pieces):
    wave = np.arange(pieces)
    signed = np.where(wave < pieces // 2, wave, wave - pieces).astype(np.float64)
    return (0.5 * (1.0 + signed / np.sqrt(signed * signed + 1.0))).astype(np.float32)


def grid_matrix(pieces, owned):
    cos_grid, sin_grid = (t.astype(np.float32) for t in dft_tables(pieces))
    parts = np.zeros((2, pieces, pieces, 2), np.float32)
    parts[0, :, :, 0] = cos_grid.T
    parts[0, :, :, 1] = sin_grid.T
    parts[1, :, :, 0] = -sin_grid.T
    parts[1, :, :, 1] = cos_grid.T
    full = np.einsum("cqir,st->scqirt", parts, np.eye(owned, dtype=np.float32))
    side = 2 * pieces * owned
    return full.reshape(side, side).astype(ml_dtypes.bfloat16)


def kernel(
    plan,
    first_ref, source_ref, opx_hbm, opy_hbm, line_hbm, grid_ref, gain_ref,
    out_ref,
    opx, opy, line, left, e_out, n_out, e_in, n_in, relay_in, d_out, d_in, nf_in, nb_in, spec, regroup,
    load_sem, e_send, e_recv, n_send, n_recv, r_send, r_recv, d_send, d_recv,
    nf_send, nf_recv, nb_send, nb_recv, s_send, s_recv,
):
    pieces, rows_by, per, group, fused = plan
    chunks = CHUNKS
    half = per * group
    width = source_ref.shape[2]
    tile = min(256, width)
    i, j = lax.axis_index("bx"), lax.axis_index("by")
    odd = lax.rem(i, 2)
    partner = i + 1 - 2 * odd
    relay_to = i - 2 + 4 * odd
    relay_from = i + 2 - 4 * odd
    has_relay_to = (relay_to >= 0) & (relay_to < pieces)
    has_relay_from = (relay_from >= 0) & (relay_from < pieces)

    loads = [
        pltpu.make_async_copy(src, dst, load_sem.at[k])
        for k, (src, dst) in enumerate(((opx_hbm, opx), (opy_hbm, opy), (line_hbm, line)))
    ]
    for load in loads:
        load.start()

    barrier = pltpu.get_barrier_semaphore()
    for k in range(1, pieces):
        pl.semaphore_signal(
            barrier, inc=1, device_id={"bx": lax.rem(i + k, pieces)}, device_id_type=MESH
        )

    @pl.when(j > 0)
    def _():
        pl.semaphore_signal(barrier, inc=1, device_id={"by": j - 1}, device_id_type=MESH)

    @pl.when(j < rows_by - 1)
    def _():
        pl.semaphore_signal(barrier, inc=1, device_id={"by": j + 1}, device_id_type=MESH)

    def clear(ref, tick, c):
        ref[tick, c] = jnp.zeros(ref.shape[2:], ref.dtype)

    def clear_all(c, _):
        clear(e_in, 0, c)
        clear(n_in, 0, c)

        @pl.when(i == 0)
        def _():
            for tick in range(1, TICKS):
                clear(e_in, tick, c)

        @pl.when(j == 0)
        def _():
            for tick in range(1, TICKS):
                clear(n_in, tick, c)
            nf_in[c] = jnp.zeros(nf_in.shape[1:], BF16)

        @pl.when(j == rows_by - 1)
        def _():
            nb_in[c] = jnp.zeros(nb_in.shape[1:], BF16)

        @pl.when(jnp.logical_not(has_relay_from))
        def _():
            relay_in[c] = jnp.zeros(relay_in.shape[1:], BF16)

        return 0

    lax.fori_loop(0, chunks, clear_all, 0)

    peers = pieces - 1 + (j > 0).astype(jnp.int32) + (j < rows_by - 1).astype(jnp.int32)
    pl.semaphore_wait(barrier, peers)

    def remote(src, dst, send, recv, where):
        return pltpu.make_async_remote_copy(
            src_ref=src, dst_ref=dst, send_sem=send, recv_sem=recv, device_id=where, device_id_type=MESH
        )

    def east(tick, c):
        return remote(
            e_out.at[tick, c], e_in.at[tick + 1, c], e_send.at[tick, c], e_recv.at[tick, c], {"bx": i + 1}
        )

    def north(tick, c):
        return remote(
            n_out.at[tick, c], n_in.at[tick + 1, c], n_send.at[tick, c], n_recv.at[tick, c], {"by": j + 1}
        )

    def relay(c):
        return remote(
            e_out.at[TICKS - 1, c], relay_in.at[c], r_send.at[c], r_recv.at[c], {"bx": relay_to}
        )

    def difference(c):
        return remote(d_out.at[c], d_in.at[c], d_send.at[c], d_recv.at[c], {"bx": partner})

    def final_north(c):
        return remote(n_out.at[TICKS - 1, c], nf_in.at[c], nf_send.at[c], nf_recv.at[c], {"by": j + 1})

    def final_south(c):
        return remote(n_out.at[TICKS - 1, c], nb_in.at[c], nb_send.at[c], nb_recv.at[c], {"by": j - 1})

    def owner(c, o):
        if o % 2 == 1 and chunks % 2 == 0:
            return c + 1 - 2 * lax.rem(c, 2) + chunks * o
        return c + chunks * o

    def regrouped(c, o):
        return remote(
            spec.at[c, o], regroup.at[i], s_send.at[c, o], s_recv.at[i], {"bx": owner(c, o)}
        )

    def shot_rows(c, o):
        return pl.ds(pl.multiple_of(owner(c, o) * group, group), group)

    def place(part, at, size, value):
        if part == 0:
            left[at : at + size, :width] = value
            left[half + at : half + at + size, width:] = value
        else:
            left[at : at + size, width:] = -value
            left[half + at : half + at + size, :width] = value

    def product(matrix, put):
        for start in range(0, width, tile):
            cols = slice(start, start + tile)
            got = jnp.dot(left[...], matrix[:, cols], preferred_element_type=F32)
            put(cols, got.astype(BF16))

    def incident(tick, c):
        active = (first_ref[0, 0] <= tick).astype(F32)
        for part in range(2):
            for o in range(per):
                at = o * group
                rows = slice(part * half + at, part * half + at + group)
                value = (
                    e_in[tick, c, rows, :].astype(F32)
                    + n_in[tick, c, rows, :].astype(F32)
                    + active * source_ref[part, shot_rows(c, o), :].astype(F32)
                )
                place(part, at, group, value.astype(BF16))

    def arrive(tick, c):
        @pl.when(i > 0)
        def _():
            east(tick - 1, c).wait_recv()

        @pl.when(j > 0)
        def _():
            north(tick - 1, c).wait_recv()

    def sweep(step, _):
        tick, c = step // chunks, lax.rem(step, chunks)

        @pl.when(tick > 0)
        def _():
            arrive(tick, c)

        incident(tick, c)

        @pl.when(step == 0)
        def _():
            loads[0].wait()

        def put_east(cols, value):
            e_out[tick, c, :, cols] = value

        product(opx, put_east)

        @pl.when(i < pieces - 1)
        def _():
            east(tick, c).start()

        @pl.when(step == 0)
        def _():
            loads[1].wait()

        def put_north(cols, value):
            n_out[tick, c, :, cols] = value

        product(opy, put_north)

        @pl.when(j < rows_by - 1)
        def _():
            north(tick, c).start()

        return 0

    lax.fori_loop(0, (TICKS - 1) * chunks, sweep, 0)
    loads[2].wait()
    last = TICKS - 1

    def last_tick(c):
        arrive(last, c)
        incident(last, c)

        def put_east(cols, value):
            e_out[last, c, :, cols] = value

        product(opx, put_east)

        @pl.when(has_relay_to)
        def _():
            relay(c).start()

        def put_north(cols, value):
            n_out[last, c, :, cols] = value

        product(opy, put_north)

        @pl.when(j < rows_by - 1)
        def _():
            final_north(c).start()

        @pl.when(j > 0)
        def _():
            final_south(c).start()

    def subtract(c):
        @pl.when(has_relay_from)
        def _():
            relay(c).wait_recv()

        sign = (2 * odd - 1).astype(F32)
        d_out[c] = (sign * (relay_in[c].astype(F32) - e_out[last, c].astype(F32))).astype(BF16)
        difference(c).start()

    def reflect(c):
        difference(c).wait_recv()

        @pl.when(j > 0)
        def _():
            final_north(c).wait_recv()

        @pl.when(j < rows_by - 1)
        def _():
            final_south(c).wait_recv()

        for part in range(2):
            rows = slice(part * half, (part + 1) * half)
            value = (
                d_in[c, rows, :].astype(F32) + nf_in[c, rows, :].astype(F32) - nb_in[c, rows, :].astype(F32)
            )
            place(part, 0, half, value.astype(BF16))

        def put_reflected(cols, value):
            d_out_free[:, cols] = value

        d_out_free = e_in.at[0, c]
        product(opx, put_reflected)
        for part in range(2):
            place(part, 0, half, d_out_free[part * half : (part + 1) * half, :])

        def put_spectrum(cols, value):
            for part in range(2):
                for o in range(per):
                    at = part * half + o * group
                    if fused:
                        spec[c, o, part * group : (part + 1) * group, cols] = value[at : at + group]
                    else:
                        out_ref[part, shot_rows(c, o), cols] = value[at : at + group]

        product(line, put_spectrum)
        if fused:
            for o in range(per):
                @pl.when(owner(c, o) == i)
                def _():
                    regroup[i] = spec[c, o]

                @pl.when(owner(c, o) != i)
                def _():
                    regrouped(c, o).start()

    def finish(step, _):
        @pl.when(step < chunks)
        def _():
            last_tick(step)

        @pl.when((step >= 1) & (step <= chunks))
        def _():
            subtract(step - 1)

        @pl.when(step >= 2)
        def _():
            reflect(step - 2)

        return 0

    lax.fori_loop(0, chunks + 2, finish, 0)

    def sent(c, _):
        for tick in range(TICKS - 1):
            @pl.when(i < pieces - 1)
            def _():
                east(tick, c).wait_send()

            @pl.when(j < rows_by - 1)
            def _():
                north(tick, c).wait_send()

        @pl.when(has_relay_to)
        def _():
            relay(c).wait_send()

        @pl.when(j < rows_by - 1)
        def _():
            final_north(c).wait_send()

        @pl.when(j > 0)
        def _():
            final_south(c).wait_send()

        difference(c).wait_send()
        return 0

    lax.fori_loop(0, chunks, sent, 0)

    if fused:
        for k in range(1, pieces):
            peer = lax.rem(i + k, pieces)
            remote(
                spec.at[0, 0], regroup.at[peer], s_send.at[0, 0], s_recv.at[peer], {"bx": peer}
            ).wait_recv()
        whole = regroup[...].reshape(2 * pieces * group, width)
        for start in range(0, width, tile):
            cols = slice(start, start + tile)
            got = jnp.dot(grid_ref[...], whole[:, cols], preferred_element_type=F32)
            out_ref[:, cols] = got * gain_ref[:, :1]
        for c in range(chunks):
            for o in range(per):
                @pl.when(owner(c, o) != i)
                def _():
                    regrouped(c, o).wait_send()


def shards(source, start_tick, op_x, op_y):
    pieces, rows_by = lax.axis_size("bx"), lax.axis_size("by")
    _, _, _, shots, width = source.shape
    owned = shots // pieces
    fused = owned % 16 == 0 and pieces % CHUNKS == 0
    per, group = (pieces // CHUNKS, owned) if fused else (1, shots // CHUNKS)
    rows = 2 * per * group
    side = 2 * pieces * owned

    cos_line, sin_line = dft_tables(width)
    line = jnp.asarray(np.concatenate([cos_line, -sin_line]))
    grid = jnp.asarray(grid_matrix(pieces, owned))
    gain = jnp.asarray(np.repeat(np.tile(grid_gain(pieces), 2 * owned)[:, None], 128, axis=1))

    vmem = pl.BlockSpec(memory_space=pltpu.VMEM)
    anywhere = pl.BlockSpec(memory_space=pl.ANY)
    out_shape = (
        jax.ShapeDtypeStruct((side, width), F32) if fused else jax.ShapeDtypeStruct((2, shots, width), BF16)
    )
    ticked = pltpu.VMEM((TICKS, CHUNKS, rows, width), BF16)
    single = pltpu.VMEM((CHUNKS, rows, width), BF16)
    operator = pltpu.VMEM((2 * width, width), BF16)
    ticked_sem = pltpu.SemaphoreType.DMA((TICKS - 1, CHUNKS))
    single_sem = pltpu.SemaphoreType.DMA((CHUNKS,))
    result = pl.pallas_call(
        functools.partial(kernel, (pieces, rows_by, per, group, fused)),
        out_shape=out_shape,
        in_specs=[pl.BlockSpec(memory_space=pltpu.SMEM), vmem, anywhere, anywhere, anywhere, vmem, vmem],
        out_specs=vmem,
        scratch_shapes=[
            operator, operator, operator,
            pltpu.VMEM((rows, 2 * width), BF16),
            ticked, ticked, ticked, ticked,
            single, single, single, single, single,
            pltpu.VMEM((CHUNKS, per, 2 * group, width), BF16),
            pltpu.VMEM((pieces, 2 * group, width) if fused else (1, 16, 128), BF16),
            pltpu.SemaphoreType.DMA((3,)),
            ticked_sem, ticked_sem, ticked_sem, ticked_sem,
            single_sem, single_sem, single_sem, single_sem,
            single_sem, single_sem, single_sem, single_sem,
            pltpu.SemaphoreType.DMA((CHUNKS, per)),
            pltpu.SemaphoreType.DMA((pieces,)),
        ],
        compiler_params=pltpu.CompilerParams(
            collective_id=0, has_side_effects=True, vmem_limit_bytes=48 * 1024 * 1024
        ),
        cost_estimate=pl.CostEstimate(
            flops=2 * rows * CHUNKS * 2 * width * width * 10, bytes_accessed=16 * width * width, transcendentals=0
        ),
    )(
        start_tick,
        source[0, 0],
        op_x.reshape(2 * width, width),
        op_y.reshape(2 * width, width),
        line,
        grid,
        gain,
    )
    if fused:
        return result.reshape(1, owned, 2, pieces, width)
    arranged = result.reshape(2, pieces, owned, 1, width)
    spectrum = lax.all_to_all(arranged, "bx", split_axis=1, concat_axis=3, tiled=True)
    received = spectrum.reshape(2, owned, pieces, width)
    cos_grid, sin_grid = (jnp.asarray(t) for t in dft_tables(pieces))

    def over_grid(values, table):
        return jnp.einsum("sik,iq->sqk", values, table, preferred_element_type=F32)

    out_real = over_grid(received[0], cos_grid) + over_grid(received[1], sin_grid)
    out_imag = over_grid(received[1], cos_grid) - over_grid(received[0], sin_grid)
    upgoing = jnp.stack([out_real, out_imag], axis=1) * grid_gain(pieces)[None, None, :, None]
    return upgoing[None]


def solution(mesh):
    placed = (
        P("bx", "by", None, None, None),
        P("bx", "by"),
        P("bx", "by", None, None, None),
        P("bx", "by", None, None, None),
    )
    return jax.shard_map(
        shards,
        mesh=mesh,
        in_specs=placed,
        out_specs=P("by", "bx", None, None, None),
        check_vma=False,
    )
```

time: 146 us -> 77.5 us (0.53)
  the two profiles are of different devices: /device:TPU:4 before, /device:TPU:26 now
where the time goes in v1:
time: 77.5 us; the launch traced here: 77.3 us
  Pallas kernels  70.6 us (91%)
  local copies, waits for them, and re-layouts  6 us (8%)
    pallas_call x1, Pallas kernels, shards(): pl.pallas_call(functools.partial(kernel, (pieces, rows_by, per, group, fu...  70.6 us
    unnamed x9, local copies, waits for them, and re-layouts  6 us

profile of v1, /device:TPU:26, one launch (start us, length us, event | category | flops | bytes accessed | tf_op | source)
XLA Modules:
  0.0 77.3 jit_solution(12379110778504534511)
XLA Ops:
  0.7 0.0 copy-start
  0.7 2.2 %copy-done = bf16[1,1,2,1024,1024]{4,3,2,1,0:T(8,128)(2,1)S(1)} copy-done((bf16[1,1,2,1024,1024]{4,3,2,1,0:T(8,128)(2,1)S(1)}, bf16[1,1,2,1024,1024]{4,3,2,1,0:T(8,128)(2,1)}, u32[]{:S(2)}) %copy-start) | copy-done | bytes 4194328
  2.8 0.0 copy-start.1
  2.8 1.0 %copy-done.1 = bf16[1,1,2,128,1024]{4,3,2,1,0:T(8,128)(2,1)S(1)} copy-done((bf16[1,1,2,128,1024]{4,3,2,1,0:T(8,128)(2,1)S(1)}, bf16[1,1,2,128,1024]{4,3,2,1,0:T(8,128)(2,1)}, u32[]{:S(2)}) %copy-start.1) | copy-done | bytes 524312
  3.9 0.0 copy-start.2
  3.9 0.9 %copy-done.2 = f32[256,128]{1,0:T(8,128)S(1)} copy-done((f32[256,128]{1,0:T(8,128)S(1)}, f32[256,128]{1,0:T(8,128)}, u32[]{:S(2)}) %copy-start.2) | copy-done | bytes 131096
  4.8 0.0 copy-start.3
  4.8 0.9 %copy-done.3 = bf16[256,256]{1,0:T(8,128)(2,1)S(1)} copy-done((bf16[256,256]{1,0:T(8,128)(2,1)S(1)}, bf16[256,256]{1,0:T(8,128)(2,1)}, u32[]{:S(2)}) %copy-start.3) | copy-done | bytes 131096
  5.7 70.6 %shard_map.73 = f32[256,1024]{1,0:T(8,128)S(1)} custom-call(s32[1,1]{1,0:T(1,128)S(6)} %copy.9.first_ref, bf16[2,128,1024]{2,1,0:T(8,128)(2,1)S(1)} %bitcast.6, bf16[2048,1024]{1,0:T(8,128)(2,1)S(1)} %bitcast.5, bf16[2048,1024]{1,0:T(8,128)(2,1)} %bitcast.7, bf16[2048,1024]{1,0:T(8,128)(2,1)} %constant.6.clone.line_hbm, bf16[256,256]{1,0:T(8,128)(2,1)S(1)} %copy-done.3, ...), custom_call_target="tpu_custom_call" | custom-call | flops 10737418240 | bytes 16777216 | tf_op jit(solution)/shard_map/pallas_call | solution.py:405
  76.3 1.0 %copy.10 = f32[1,16,2,8,1024]{4,3,2,1,0:T(8,128)} copy(f32[1,16,2,8,1024]{4,3,2,1,0:T(8,128)S(1)} %bitcast.4) | data formatting | bytes 2097152
Async XLA Ops:
  0.7 2.2 %copy-start = (bf16[1,1,2,1024,1024]{4,3,2,1,0:T(8,128)(2,1)S(1)}, bf16[1,1,2,1024,1024]{4,3,2,1,0:T(8,128)(2,1)}, u32[]{:S(2)}) copy-start(bf16[1,1,2,1024,1024]{4,3,2,1,0:T(8,128)(2,1)} %param.9) | copy-start | bytes 12582916
  2.8 1.0 %copy-start.1 = (bf16[1,1,2,128,1024]{4,3,2,1,0:T(8,128)(2,1)S(1)}, bf16[1,1,2,128,1024]{4,3,2,1,0:T(8,128)(2,1)}, u32[]{:S(2)}) copy-start(bf16[1,1,2,128,1024]{4,3,2,1,0:T(8,128)(2,1)} %param.7) | copy-start | bytes 1572868
  3.9 0.9 %copy-start.2 = (f32[256,128]{1,0:T(8,128)S(1)}, f32[256,128]{1,0:T(8,128)}, u32[]{:S(2)}) copy-start(f32[256,128]{1,0:T(8,128)} %constant.8.clone.gain_ref) | copy-start | bytes 393220
  4.8 0.9 %copy-start.3 = (bf16[256,256]{1,0:T(8,128)(2,1)S(1)}, bf16[256,256]{1,0:T(8,128)(2,1)}, u32[]{:S(2)}) copy-start(bf16[256,256]{1,0:T(8,128)(2,1)} %constant.7.clone.grid_ref) | copy-start | bytes 393220
